TPU v7x, 512 devices: a whole 4x4x16 slice. The times are simulated.
512 devices in a mesh: dom: 64 (over x, z), sub: 8 (over y, core).
Axes of the slice: x: 4, y: 4, z: 16, core: 2. Of those that a mesh axis runs over, the one named last changes fastest.
Arguments:
- right_side: float32 [1024, 16, 128], P(('dom', 'sub')), as said below
- diag_blocks: float32 [1024, 128, 128], P(('dom', 'sub')), as said below
- block_values: float32 [1024, 4, 128, 128], P(('dom', 'sub')), as said below
- block_cols: int32 [1024, 4], P(('dom', 'sub')), may hold values from 0 to 31, as said below
- block_count: int32 [1024], P(('dom', 'sub')), may hold values from 0 to 4, as said below
- cell_diagonal: float32 [1024, 128], P(('dom', 'sub')), as said below
Outputs:
- solution_field: float32 [1024, 16, 128], P(('dom', 'sub'))
- residual: float32 [1024, 16, 128], P(('dom', 'sub'))
Inputs may be any that keep to these rules, and one draw needn't show every extreme that they name: `block_cols`: live slots of a block row point to distinct block rows that come after it in the window (positions 0 to 15 are the block rows of the same index of dom, the rest those of the next index); block rows of the last index of dom point only into their own index; dead slots hold 0. `block_count`: the number of live slots, which varies from device to device. `block_values`: entries lie between -1 / 128 and 0. `diag_blocks`: entries lie between -1 / 128 and 0. `cell_diagonal`: every entry exceeds 1 + the live slots of its block row + the live slots of all block rows that couple to its block row, so the operator is strictly diagonally dominant. `right_side`: entries lie between -50 and 50.
All inputs are finite; a program needn't handle non-finite values.
Results may differ from a plain program's by a relative error of at most 0.00065.
Values sent between devices are 32-bit elements; how exact they have to be, the bound alone decides.
A program may use at most 64 MiB of HBM per device.

v0:
```python
import jax
import jax.numpy as jnp
from jax import lax
from jax.sharding import PartitionSpec as P

K = 4
ITERS = 3


PRECISE = lax.Precision.HIGHEST


def passed_along(x, axis, by):
    peers = lax.axis_size(axis)
    pairs = [(i, i + by) for i in range(peers) if 0 <= i + by < peers]
    return lax.ppermute(x, axis, pairs)


def local(right_side, diag_blocks, block_values, block_cols, block_count, cell_diagonal):
    rows_dev = right_side.shape[0]
    group_rows = lax.axis_size("sub") * rows_dev
    upper_part = jnp.triu(diag_blocks, 1)
    live_slots = jnp.arange(K, dtype=jnp.int32)[None, :] < block_count[:, None]
    window_ids = jnp.arange(2 * group_rows, dtype=jnp.int32)
    picker = (
        (block_cols[:, :, None] == window_ids[None, None, :]) & live_slots[:, :, None]
    ).astype(jnp.float32)

    def local_dots(first, second):
        return jnp.sum(first * second, axis=(0, 2))

    def residual_sum(residual_now, precond_now):
        return lax.psum(local_dots(residual_now, precond_now), ("dom", "sub"))

    solution_field = jnp.zeros_like(right_side)
    residual = right_side
    precond_res = residual / cell_diagonal[:, None, :]
    direction = precond_res
    precond_dot = residual_sum(residual, precond_res)
    for iteration in range(ITERS):
        own_part = jnp.einsum("rab,rzb->rza", upper_part, direction, precision=PRECISE)
        own_part = own_part + jnp.einsum("rba,rzb->rza", upper_part, direction, precision=PRECISE)
        own_part = own_part + cell_diagonal[:, None, :] * direction
        own_group = lax.all_gather(direction, "sub", axis=0, tiled=True)
        next_group = passed_along(own_group, "dom", -1)
        window = jnp.concatenate([own_group, next_group], axis=0)
        far_rows = jnp.einsum("rkw,wzb->rkzb", picker, window, precision=PRECISE)
        forward = jnp.einsum("rkab,rkzb->rza", block_values, far_rows, precision=PRECISE)
        back_terms = jnp.einsum("rkba,rzb->rkza", block_values, direction, precision=PRECISE)
        spread = jnp.einsum("rkw,rkza->wza", picker, back_terms, precision=PRECISE)
        incoming = passed_along(spread[group_rows:], "dom", 1)
        back_own = lax.psum_scatter(
            spread[:group_rows] + incoming, "sub", scatter_dimension=0, tiled=True
        )
        image_vec = own_part + forward + back_own
        curvature = lax.psum(local_dots(direction, image_vec), ("dom", "sub"))
        step_size = precond_dot / curvature
        solution_field = solution_field + step_size[None, :, None] * direction
        residual = residual - step_size[None, :, None] * image_vec
        if iteration + 1 < ITERS:
            precond_res = residual / cell_diagonal[:, None, :]
            new_dot = residual_sum(residual, precond_res)
            direction = precond_res + (new_dot / precond_dot)[None, :, None] * direction
            precond_dot = new_dot
    return (solution_field, residual)


def solution(mesh):
    return jax.shard_map(
        local,
        mesh=mesh,
        in_specs=(
            P(("dom", "sub"), None, None),
            P(("dom", "sub"), None, None),
            P(("dom", "sub"), None, None, None),
            P(("dom", "sub"), None),
            P(("dom", "sub")),
            P(("dom", "sub"), None),
        ),
        out_specs=(P(("dom", "sub"), None, None), P(("dom", "sub"), None, None)),
        check_vma=False,
    )
```

profile of v0, /device:TPU:1, one launch (start us, length us, event | category | flops | bytes accessed | tf_op | source)
XLA Modules:
  0.0 715.4 jit_solution(11586665640421009732)
XLA Ops:
  7.2 0.8 broadcast_divide_fusion
  8.0 19.6 %all_gather.9 = f32[16,16,128]{2,1,0:T(8,128)S(1)} all-gather(f32[2,16,128]{2,1,0:T(8,128)S(1)} %broadcast_divide_fusion), channel_id=1, replica_groups=mesh['dom'=64,'sub'=8] {'sub'}, dimensions={0}, use_global_device_ids=true | all-gather | bytes 147456 | tf_op jit(solution)/shard_map/all_gather | solution.py:44
  27.6 1.4 collective-permute-start
  29.1 0.4 fusion.46
  29.5 0.3 copy-done.4
  29.8 0.4 convolution_bitcast_fusion.2
  30.3 4.0 collective-permute-start.1
  34.3 0.3 fusion.19
  34.7 0.3 fusion.10
  35.0 1.7 collective-permute-done.1
  36.7 0.7 copy_add_fusion.2
  37.5 0.5 convolution_bitcast_fusion.5
  38.0 0.2 fusion.5
  38.2 37.2 %reduce-scatter.4.cloned.1.call-done = f32[2,16,128]{2,1,0:T(8,128)} async-done(((f32[16,16,128]{2,1,0:T(8,128)}), f32[2,16,128]{2,1,0:T(8,128)}) %reduce-scatter.4.cloned.1.call-update) | async-done | bytes 16400 | tf_op jit(solution)/shard_map/reduce_scatter | solution.py:52
  75.4 0.8 multiply_reduce_fusion.4
  76.2 105.7 %all-reduce = (f32[16]{0:T(128)S(1)}, f32[16]{0:T(128)S(1)}) all-reduce(f32[16]{0:T(128)S(1)} %get-tuple-element.3, f32[16]{0:T(128)S(1)} %get-tuple-element.2), channel_id=1, replica_groups=mesh['dom'=64,'sub'=8] {'dom','sub'}, use_global_device_ids=true, to_apply=%region_1.2 | all-reduce | flops 32 | bytes 256 | tf_op jit(solution)/shard_map/psum | solution.py:33
  182.2 99.4 %psum.44 = f32[16]{0:T(128)S(1)} all-reduce(f32[16]{0:T(128)S(1)} %get-tuple-element.12), channel_id=1, replica_groups=mesh['dom'=64,'sub'=8] {'dom','sub'}, use_global_device_ids=true, to_apply=%region_6.7 | all-reduce | flops 16 | bytes 128 | tf_op jit(solution)/shard_map/psum | solution.py:33
  281.7 13.2 %all_gather.10 = f32[16,16,128]{2,1,0:T(8,128)S(1)} all-gather(f32[2,16,128]{2,1,0:T(8,128)S(1)} %multiply_add_fusion.2), channel_id=1, replica_groups=mesh['dom'=64,'sub'=8] {'sub'}, dimensions={0}, use_global_device_ids=true | all-gather | bytes 147456 | tf_op jit(solution)/shard_map/all_gather | solution.py:44
  294.9 0.4 fusion.44
  295.3 1.3 collective-permute-start.2
  296.6 0.4 convolution_bitcast_fusion.1
  297.1 4.0 collective-permute-start.3
  301.1 0.3 fusion.16
  301.3 0.7 collective-permute-done.2
  302.1 0.3 fusion.8
  302.4 1.0 collective-permute-done.3
  303.4 0.7 copy_add_fusion.1
  304.2 0.5 convolution_bitcast_fusion.4
  304.7 0.2 fusion.3
  305.0 33.6 %reduce-scatter.6.cloned.1.call-done = f32[2,16,128]{2,1,0:T(8,128)} async-done(((f32[16,16,128]{2,1,0:T(8,128)}), f32[2,16,128]{2,1,0:T(8,128)}) %reduce-scatter.6.cloned.1.call-update) | async-done | bytes 16400 | tf_op jit(solution)/shard_map/reduce_scatter | solution.py:52
  338.5 0.8 multiply_reduce_fusion.2
  339.4 105.7 %psum.45 = f32[16]{0:T(128)S(1)} all-reduce(f32[16]{0:T(128)S(1)} %get-tuple-element.10), channel_id=1, replica_groups=mesh['dom'=64,'sub'=8] {'dom','sub'}, use_global_device_ids=true, to_apply=%region_9.10 | all-reduce | flops 16 | bytes 128 | tf_op jit(solution)/shard_map/psum | solution.py:56
  445.3 99.2 %psum.46 = f32[16]{0:T(128)S(1)} all-reduce(f32[16]{0:T(128)S(1)} %get-tuple-element.8), channel_id=1, replica_groups=mesh['dom'=64,'sub'=8] {'dom','sub'}, use_global_device_ids=true, to_apply=%region_11.12 | all-reduce | flops 16 | bytes 128 | tf_op jit(solution)/shard_map/psum | solution.py:33
  544.6 13.2 %all_gather.11 = f32[16,16,128]{2,1,0:T(8,128)S(1)} all-gather(f32[2,16,128]{2,1,0:T(8,128)S(1)} %multiply_add_fusion.1), channel_id=1, replica_groups=mesh['dom'=64,'sub'=8] {'sub'}, dimensions={0}, use_global_device_ids=true | all-gather | bytes 147456 | tf_op jit(solution)/shard_map/all_gather | solution.py:44
  557.8 0.4 fusion.42
  558.2 1.3 collective-permute-start.4
  559.5 0.4 convolution_bitcast_fusion
  560.0 4.0 collective-permute-start.5
  564.0 0.3 fusion.13
  564.2 0.7 collective-permute-done.4
  565.0 0.3 fusion.6
  565.3 1.0 collective-permute-done.5
  566.3 0.7 copy_add_fusion
  567.1 0.5 convolution_bitcast_fusion.3
  567.8 33.7 %reduce-scatter.8.cloned.1.call-done = f32[2,16,128]{2,1,0:T(8,128)} async-done(((f32[16,16,128]{2,1,0:T(8,128)}), f32[2,16,128]{2,1,0:T(8,128)}) %reduce-scatter.8.cloned.1.call-update) | async-done | bytes 16400 | tf_op jit(solution)/shard_map/reduce_scatter | solution.py:52
  601.5 0.8 multiply_reduce_fusion
  602.4 105.8 %psum.47 = f32[16]{0:T(128)S(1)} all-reduce(f32[16]{0:T(128)S(1)} %get-tuple-element.6), channel_id=1, replica_groups=mesh['dom'=64,'sub'=8] {'dom','sub'}, use_global_device_ids=true, to_apply=%region_14.15 | all-reduce | flops 16 | bytes 128 | tf_op jit(solution)/shard_map/psum | solution.py:56
  708.2 0.7 multiply_subtract_fusion
  (39 shorter events, 1.3 us)
Async XLA Ops:
  7.2 21.9 %copy-start = (f32[2,4,128,128]{3,2,1,0:T(8,128)S(1)}, f32[2,4,128,128]{3,2,1,0:T(8,128)}, u32[]{:S(2)}) copy-start(f32[2,4,128,128]{3,2,1,0:T(8,128)} %param.8) | copy-start | bytes 1572868
  7.2 68.2 %reduce-scatter.4.cloned.1.call-start = ((), (), s32[]{:S(2)}) async-start(), calls=%async_computation.3 | async-start | bytes 147456 | tf_op jit(solution)/shard_map/reduce_scatter | solution.py:52
  8.0 21.0 %copy-start.5 = (s32[2]{0:T(128)S(1)}, s32[2]{0:T(128)}, u32[]{:S(2)}) copy-start(s32[2]{0:T(128)} %param.10) | copy-start | bytes 28
  8.0 21.1 %copy-start.2 = (f32[2,16,128]{2,1,0:T(8,128)S(1)}, f32[2,16,128]{2,1,0:T(8,128)}, u32[]{:S(2)}) copy-start(f32[2,16,128]{2,1,0:T(8,128)} %param.6) | copy-start | bytes 49156
  27.6 1.5 copy-start.3
  27.6 7.0 collective-permute-start
  29.1 0.7 copy-start.4
  30.2 4.1 copy-start.1
  30.3 6.4 collective-permute-start.1
  37.4 301.1 %reduce-scatter.6.cloned.1.call-start = ((), (), s32[]{:S(2)}) async-start(), calls=%async_computation.4 | async-start | bytes 147456 | tf_op jit(solution)/shard_map/reduce_scatter | solution.py:52
  295.3 6.8 collective-permute-start.2
  297.1 6.4 collective-permute-start.3
  304.2 297.4 %reduce-scatter.8.cloned.1.call-start = ((), (), s32[]{:S(2)}) async-start(), calls=%async_computation.5 | async-start | bytes 147456 | tf_op jit(solution)/shard_map/reduce_scatter | solution.py:52
  558.2 6.8 collective-permute-start.4
  560.0 6.4 collective-permute-start.5
Sparse Core Ops, SparseCore 0:
  37.5 37.8 reduce-scatter.3
  304.3 34.2 reduce-scatter.5
  567.2 34.3 reduce-scatter.7
where the time goes:
time: 717 us; the launch traced here: 715 us
  blocking collectives  562 us (78%)
  waiting for transfers between devices  110 us (15%)
  starting transfers between devices  16.1 us (2%)
  between operations  14 us (2%)
    psum x3, blocking collectives, residual_sum(): return lax.psum(local_dots(residual_now, precond_now), ('dom', 'sub'))  304 us
    psum x2, blocking collectives, local(): curvature = lax.psum(local_dots(direction, image_vec), ('dom', 'sub'))  212 us
    reduce_scatter x3, waiting for transfers between devices, local(): lax.psum_scatter(spread[:group_rows] + incoming, 'sub', scatter_dimension...  104 us
    all_gather x3, blocking collectives, local(): own_group = lax.all_gather(direction, 'sub', axis=0, tiled=True)  46.1 us
    ppermute x6, starting transfers between devices, passed_along(): return lax.ppermute(x, axis, pairs)  16 us
  transfers between devices with their start and end apart: 9, of which 8 were waited for; matrix products, arithmetic and copies ran while one was open for 1% of the time, Pallas kernels for 0%

commit v1 on v0

v1 whole, which is shorter than its diff:
```python
import functools

import jax
import jax.numpy as jnp
from jax import lax
from jax.experimental import pallas as pl
from jax.experimental.pallas import tpu as pltpu
from jax.sharding import PartitionSpec as P

MESH = pl.DeviceIdType.MESH
K = 4
ITERS = 3
BS = 128
HALF = 8
X, Y, Z = 4, 4, 16
N_DOM = X * Z
GROUP = 4 * Y
F32, BF16, I32 = jnp.float32, jnp.bfloat16, jnp.int32


def ring_order(n):
    return sorted(range(1, n), key=lambda d: -min(d, n - d))


def split(v):
    high = v.astype(BF16).astype(F32)
    return jnp.concatenate([high, v - high], axis=0).astype(BF16)


def kernel(
    right_ref, diag_ref, blocks_ref, cols_ref, count_ref, celld_ref,
    x_out, res_out,
    rhs, dst, diag_in, dcell, sym, blocks, table_v, table_w, place_s, slot_s, w_off, w_sym,
    mine, win_0, win_1, win_2, prods, spread, tin, red_src, red_a, red_b, outs,
    local_sems, pair_send, pair_recv, ex_send, ex_recv, red_send, red_recv,
):
    dom, sub = lax.axis_index("dom"), lax.axis_index("sub")
    xx, zz = dom // Z, lax.rem(dom, Z)
    yy, core = sub // 2, lax.rem(sub, 2)
    other = 1 - core
    own = pl.ds(2 * core, 2)
    theirs = pl.ds(2 * other, 2)
    partner = (dom, 2 * yy + other)

    def at(dx, dy, dz):
        return (
            lax.rem(xx + dx, X) * Z + lax.rem(zz + dz, Z),
            2 * lax.rem(yy + dy, Y) + core,
        )

    def dom_at(step, dy):
        return (lax.rem(dom + step + N_DOM, N_DOM), 2 * lax.rem(yy + dy, Y) + core)

    loads = [
        pltpu.make_async_copy(celld_ref, dcell, local_sems.at[0]),
        pltpu.make_async_copy(right_ref.at[:, pl.ds(HALF * core, HALF)], rhs.at[own], local_sems.at[1]),
        pltpu.make_async_copy(diag_ref, diag_in, local_sems.at[2]),
        pltpu.make_async_copy(blocks_ref, blocks.at[own], local_sems.at[3]),
    ]
    for load in loads:
        load.start()

    win = (win_0, win_1, win_2)
    for window in win:
        window[...] = jnp.zeros_like(window)
    tin[...] = jnp.zeros_like(tin)

    barrier = pltpu.get_barrier_semaphore()
    plane = [(dx, dy) for dx in range(X) for dy in range(Y) if dx or dy]
    plane.sort(key=lambda p: -(min(p[0], X - p[0]) + min(p[1], Y - p[1])))
    greet = [partner]
    greet += [at(0, 0, dz) for dz in ring_order(Z)]
    greet += [at(dx, dy, 0) for dx, dy in plane]
    greet += [dom_at(step, dy) for step in (1, -1) for dy in range(Y)]
    for device in greet:
        pl.semaphore_signal(barrier, inc=1, device_id=device, device_id_type=MESH)

    for h in range(4):
        prods[5 * h + K] = jnp.zeros((HALF, BS), F32)
    lane = lax.broadcasted_iota(I32, (1, BS), 1)
    places = []
    for i in range(2):
        row = jnp.zeros((1, BS), I32)
        for k in range(K):
            place = jnp.where(k < count_ref[i], cols_ref[i, k], 2 * GROUP)
            row = jnp.where(lane == k, place, row)
            places.append(place)
        table_v[i : i + 1, :] = row
    table_v[2:8, :] = jnp.zeros((6, BS), I32)

    def tabulate(base, places):
        for i in range(2):
            for k in range(K):
                place_s[(base + i) * K + k] = places[i * K + k]
            for w in range(2 * GROUP):
                slot = K
                for k in range(K):
                    slot = jnp.where(places[i * K + k] == w, k, slot)
                slot_s[(base + i) * 2 * GROUP + w] = slot + (base + i) * (K + 1)

    tabulate(2 * core, places)

    loads[0].wait()
    for i in range(2):
        dst[2 * core + i] = jnp.broadcast_to(dcell[i : i + 1, :], (HALF, BS))
    loads[2].wait()
    upper = lax.broadcasted_iota(I32, (BS, BS), 0) < lax.broadcasted_iota(I32, (BS, BS), 1)
    for i in range(2):
        part = jnp.where(upper, diag_in[i], 0.0)
        sym[2 * core + i] = part + part.T

    pl.semaphore_wait(barrier, len(greet))

    def to_partner(index, source, target):
        copy = pltpu.make_async_remote_copy(
            src_ref=source, dst_ref=target, send_sem=pair_send.at[index], recv_sem=pair_recv.at[index],
            device_id=partner, device_id_type=MESH,
        )
        copy.start()
        return copy

    pair = [
        to_partner(0, right_ref.at[:, pl.ds(HALF * other, HALF)], rhs.at[own]),
        to_partner(1, dst.at[own], dst.at[own]),
        to_partner(2, table_v, table_w),
        to_partner(3, blocks_ref, blocks.at[own]),
        to_partner(4, sym.at[own], sym.at[own]),
    ]

    def widen(h):
        for k in range(K):
            block = blocks[h, k]
            high = block.astype(BF16)
            w_off[h, 0:BS, k * BS : (k + 1) * BS] = high
            w_off[h, BS : 2 * BS, k * BS : (k + 1) * BS] = (block - high.astype(F32)).astype(BF16)

    def widen_sym(h):
        high = sym[h].astype(BF16)
        w_sym[h, 0:BS, :] = high
        w_sym[h, BS : 2 * BS, :] = (sym[h] - high.astype(F32)).astype(BF16)

    loads[1].wait()
    pair[0].wait_recv()
    pair[1].wait_recv()
    inverse = [1.0 / dst[h] for h in range(4)]
    u = [[rhs[h] * inverse[h] for h in range(4)]]
    image = []

    def exchange(index, j, source, target, device):
        return pltpu.make_async_remote_copy(
            src_ref=source, dst_ref=target, send_sem=ex_send.at[j, index], recv_sem=ex_recv.at[j, index],
            device_id=device, device_id_type=MESH,
        )

    def await_bytes(sem, buffer):
        pltpu.make_async_copy(buffer, buffer, sem).wait()

    def send_field(j):
        @pl.when(dom > 0)
        def _():
            for dy in (2, 1, 3, 0):
                exchange(0, j, mine.at[j], win[j].at[pl.ds(GROUP + 4 * yy, 4)], dom_at(-1, dy)).start()

        for y_here in range(1, Y):
            @pl.when(yy == y_here)
            def _():
                for y_there in range(y_here):
                    exchange(
                        1, j, mine.at[j], win[j].at[pl.ds(4 * y_here, 4)], (dom, 2 * y_there + core)
                    ).start()

    def send_products(j):
        @pl.when(dom < N_DOM - 1)
        def _():
            for dy in (2, 1, 3, 0):
                rows = pl.ds(GROUP + 4 * lax.rem(yy + dy, Y), 4)
                exchange(2, j, spread.at[j, rows], tin.at[j, Y + yy], dom_at(1, dy)).start()

        for y_here in range(Y - 1):
            @pl.when(yy == y_here)
            def _():
                for y_there in range(y_here + 1, Y):
                    exchange(
                        3, j, spread.at[j, pl.ds(4 * y_there, 4)], tin.at[j, y_here], (dom, 2 * y_there + core)
                    ).start()

    def await_field(j):
        for y_here in range(Y - 1):
            @pl.when(yy == y_here)
            def _():
                await_bytes(ex_recv.at[j, 1], win[j].at[pl.ds(0, 4 * (Y - 1 - y_here))])

        @pl.when(dom < N_DOM - 1)
        def _():
            await_bytes(ex_recv.at[j, 0], win[j].at[pl.ds(GROUP, GROUP)])

    def await_products(j):
        for y_here in range(1, Y):
            @pl.when(yy == y_here)
            def _():
                await_bytes(ex_recv.at[j, 3], win[j].at[pl.ds(0, 4 * y_here)])

        @pl.when(dom > 0)
        def _():
            await_bytes(ex_recv.at[j, 2], win[j].at[pl.ds(GROUP, GROUP)])

    def await_sends(j):
        @pl.when(dom > 0)
        def _():
            await_bytes(ex_send.at[j, 0], win[j].at[pl.ds(GROUP, GROUP)])

        @pl.when(dom < N_DOM - 1)
        def _():
            await_bytes(ex_send.at[j, 2], win[j].at[pl.ds(GROUP, GROUP)])

        for y_here in range(Y):
            @pl.when(yy == y_here)
            def _():
                if y_here:
                    await_bytes(ex_send.at[j, 1], win[j].at[pl.ds(0, 4 * y_here)])
                if y_here < Y - 1:
                    await_bytes(ex_send.at[j, 3], win[j].at[pl.ds(0, 4 * (Y - 1 - y_here))])

    def fold(out):
        return (out[0:HALF, 0:BS] + out[0:HALF, BS:]) + (out[HALF:, 0:BS] + out[HALF:, BS:])

    across = (((1,), (1,)), ((), ()))
    terms = []
    terms.append(sum(rhs[h] * u[0][h] for h in range(4)))

    for j in range(ITERS):
        field = u[j]
        for h in range(4):
            mine[j, h] = field[h]
            win[j][4 * yy + h] = field[h]
        send_field(j)
        parts = [split(field[h]) for h in range(4)]
        if j == 0:
            loads[3].wait()
            pair[2].wait_recv()
            rows = table_w[...]
            tabulate(2 * other, [rows[i, k] for i in range(2) for k in range(K)])
            pair[3].wait_recv()
            for h in range(4):
                widen(h)
        for h in range(4):
            out = jnp.dot(
                jnp.concatenate([parts[h], parts[h]], axis=1), w_off[h], preferred_element_type=F32
            )
            for k in range(K):
                prods[5 * h + k] = out[0:HALF, k * BS : (k + 1) * BS] + out[HALF:, k * BS : (k + 1) * BS]
        for w in range(2 * GROUP):
            picked = [prods[slot_s[h * 2 * GROUP + w]] for h in range(4)]
            spread[j, w] = (picked[0] + picked[1]) + (picked[2] + picked[3])
        send_products(j)
        if j == 0:
            pair[4].wait_recv()
            for h in range(4):
                widen_sym(h)
        near = [
            fold(lax.dot_general(parts[h], w_sym[h], across, preferred_element_type=F32)) for h in range(4)
        ]
        await_field(j)
        ahead = []
        for h in range(4):
            tiles = [split(win[j][place_s[h * K + k]]) for k in range(K)]
            ahead.append(
                fold(
                    lax.dot_general(
                        jnp.concatenate(tiles, axis=1), w_off[h], across, preferred_element_type=F32
                    )
                )
            )
        if j == ITERS - 1:
            terms.append(sum(field[h] * (2.0 * ahead[h] + near[h]) for h in range(4)))
        else:
            await_products(j)
            applied = []
            for h in range(4):
                back = spread[j, 4 * yy + h]
                for s in range(2 * Y):
                    back = back + tin[j, s, h]
                applied.append(near[h] + ahead[h] + back)
            image.append(applied)
            u.append([applied[h] * inverse[h] for h in range(4)])
            terms.append(sum(field[h] * applied[h] for h in range(4)))
            terms.append(sum(u[j + 1][h] * applied[h] for h in range(4)))

    lanes = lax.broadcasted_iota(I32, (HALF, BS), 1)
    tile = jnp.zeros((HALF, BS), F32)
    for index, term in enumerate(terms):
        tile = jnp.where(lanes == index, jnp.sum(term, axis=1, keepdims=True), tile)

    def reduced(stage, buffer, slot, devices, tile):
        red_src[stage] = tile
        buffer[slot] = tile
        for device in devices:
            pltpu.make_async_remote_copy(
                src_ref=red_src.at[stage], dst_ref=buffer.at[slot], send_sem=red_send.at[stage],
                recv_sem=red_recv.at[stage], device_id=device, device_id_type=MESH,
            ).start()

    def total(stage, buffer, count):
        await_bytes(red_recv.at[stage], buffer.at[pl.ds(0, count - 1)])
        values = [buffer[i] for i in range(count)]
        while len(values) > 1:
            values = [values[i] + values[i + 1] for i in range(0, len(values), 2)]
        return values[0]

    reduced(0, red_a, Y * xx + yy, [at(dx, dy, 0) for dx, dy in plane], tile)
    last = ITERS - 1
    await_products(last)
    applied = []
    for h in range(4):
        back = spread[last, 4 * yy + h]
        for s in range(2 * Y):
            back = back + tin[last, s, h]
        applied.append(near[h] + ahead[h] + back)
    image.append(applied)
    tile = total(0, red_a, X * Y)
    reduced(1, red_b, zz, [at(0, 0, dz) for dz in ring_order(Z)], tile)
    tile = total(1, red_b, Z)

    gram = [jnp.broadcast_to(tile[:, i : i + 1], (HALF, BS)) for i in range(2 * ITERS)]

    def inner(a, b):
        value = None
        for i in range(len(a)):
            for k in range(len(b)):
                if a[i] is not None and b[k] is not None:
                    term = a[i] * b[k] * gram[i + k]
                    value = term if value is None else value + term
        return value

    def plus(a, b):
        return a if b is None else b if a is None else a + b

    one = jnp.ones((HALF, BS), F32)
    zc, pc, xc = [one, None, None, None], [one, None, None], [None, None, None]
    rho = gram[0]
    for step in range(ITERS):
        ac = [pc[0], plus(pc[1], pc[0]), plus(pc[2], pc[1]), pc[2]]
        alpha = rho / inner(pc, ac)
        xc = [plus(xc[i], None if pc[i] is None else alpha * pc[i]) for i in range(3)]
        zc = [plus(zc[i], None if ac[i] is None else -alpha * ac[i]) for i in range(4)]
        if step < ITERS - 1:
            fresh = inner(zc, zc)
            beta = fresh / rho
            pc = [plus(zc[i], None if pc[i] is None else beta * pc[i]) for i in range(3)]
            rho = fresh

    for h in range(4):
        outs[0, h] = xc[0] * u[0][h] + xc[1] * u[1][h] + xc[2] * u[2][h]
        outs[1, h] = zc[0] * rhs[h] + zc[1] * image[0][h] + zc[2] * image[1][h] + zc[3] * image[2][h]

    mine_half = pl.ds(HALF * core, HALF)
    ends = []
    for i, out in enumerate((x_out, res_out)):
        ends.append(to_partner(5 + i, outs.at[i, theirs], out.at[:, mine_half]))
        keep = pltpu.make_async_copy(outs.at[i, own], out.at[:, mine_half], local_sems.at[5 + i])
        keep.start()
        ends.append(keep)
    for j in range(ITERS):
        await_sends(j)
    await_bytes(red_send.at[0], red_a.at[pl.ds(0, X * Y - 1)])
    await_bytes(red_send.at[1], red_b.at[pl.ds(0, Z - 1)])
    for copy in pair:
        copy.wait_send()
    for copy in ends:
        copy.wait()


def local(right_side, diag_blocks, block_values, block_cols, block_count, cell_diagonal):
    hbm = pl.BlockSpec(memory_space=pl.ANY)
    smem = pl.BlockSpec(memory_space=pltpu.SMEM)
    shape = jax.ShapeDtypeStruct(right_side.shape, F32)
    return pl.pallas_call(
        kernel,
        out_shape=(shape, shape),
        in_specs=[hbm, hbm, hbm, smem, smem, hbm],
        out_specs=(hbm, hbm),
        scratch_shapes=[
            pltpu.VMEM((4, HALF, BS), F32),
            pltpu.VMEM((4, HALF, BS), F32),
            pltpu.VMEM((2, BS, BS), F32),
            pltpu.VMEM((2, BS), F32),
            pltpu.VMEM((4, BS, BS), F32),
            pltpu.VMEM((4, K, BS, BS), F32),
            pltpu.VMEM((8, BS), I32),
            pltpu.VMEM((8, BS), I32),
            pltpu.SMEM((4 * K,), I32),
            pltpu.SMEM((4 * 2 * GROUP,), I32),
            pltpu.VMEM((4, 2 * BS, K * BS), BF16),
            pltpu.VMEM((4, 2 * BS, BS), BF16),
            pltpu.VMEM((ITERS, 4, HALF, BS), F32),
            pltpu.VMEM((2 * GROUP + 1, HALF, BS), F32),
            pltpu.VMEM((2 * GROUP + 1, HALF, BS), F32),
            pltpu.VMEM((2 * GROUP + 1, HALF, BS), F32),
            pltpu.VMEM((4 * (K + 1), HALF, BS), F32),
            pltpu.VMEM((ITERS, 2 * GROUP, HALF, BS), F32),
            pltpu.VMEM((ITERS, 2 * Y, 4, HALF, BS), F32),
            pltpu.VMEM((2, HALF, BS), F32),
            pltpu.VMEM((X * Y, HALF, BS), F32),
            pltpu.VMEM((Z, HALF, BS), F32),
            pltpu.VMEM((2, 4, HALF, BS), F32),
            pltpu.SemaphoreType.DMA((7,)),
            pltpu.SemaphoreType.DMA((7,)),
            pltpu.SemaphoreType.DMA((7,)),
            pltpu.SemaphoreType.DMA((ITERS, 4)),
            pltpu.SemaphoreType.DMA((ITERS, 4)),
            pltpu.SemaphoreType.DMA((2,)),
            pltpu.SemaphoreType.DMA((2,)),
        ],
        compiler_params=pltpu.CompilerParams(
            collective_id=0, has_side_effects=True, vmem_limit_bytes=24 << 20
        ),
        name="cg",
    )(right_side, diag_blocks, block_values, block_cols, block_count, cell_diagonal)


def solution(mesh):
    rows = P(("dom", "sub"))
    return jax.shard_map(
        local,
        mesh=mesh,
        in_specs=(rows,) * 6,
        out_specs=(rows, rows),
        check_vma=False,
    )
```

time: 717 us -> 53.9 us (0.08)
  blocking collectives: 562 us -> 0 us
  waiting for transfers between devices: 110 us -> 0 us
  Pallas kernels: 0 us -> 47.1 us
  starting transfers between devices: 16.1 us -> 0 us
  between operations: 14 us -> 0.65 us
    psum x5 -> x0, blocking collectives: 516 us -> none  [the longest x3 304 us: residual_sum(): return lax.psum(local_dots(residual_now, precond_now), ('dom', 'sub'))]
    reduce_scatter x3 -> x0, waiting for transfers between devices: 104 us -> none  [local(): lax.psum_scatter(spread[:group_rows] + incoming, 'sub', scatter_dimension...]
    pallas_call x0 -> x1, Pallas kernels: none -> 47.1 us  [local(): pl.pallas_call(kernel, out_shape=(shape, shape), in_specs=[hbm, hbm, hbm,...]
    all_gather x3 -> x0, blocking collectives: 46.1 us -> none  [local(): own_group = lax.all_gather(direction, 'sub', axis=0, tiled=True)]
    ppermute x6 -> x0, starting transfers between devices: 16 us -> none  [passed_along(): return lax.ppermute(x, axis, pairs)]
  transfers between devices with their start and end apart: 9 -> 0, of which waited for: 8 -> 0; matrix products, arithmetic and copies ran while one was open for 1% -> 0% of each run, Pallas kernels for 0% -> 0%
where the time goes in v1:
time: 53.9 us; the launch traced here: 53.6 us
  Pallas kernels  47.1 us (87%)
  local copies, waits for them, and re-layouts  5.88 us (11%)
  between operations  0.65 us (1%)
    pallas_call x1, Pallas kernels, local(): pl.pallas_call(kernel, out_shape=(shape, shape), in_specs=[hbm, hbm, hbm,...  47.1 us
    unnamed x14, local copies, waits for them, and re-layouts  5.88 us

profile of v1, /device:TPU:1, one launch (start us, length us, event | category | flops | bytes accessed | tf_op | source)
XLA Modules:
  0.0 53.6 jit_solution(3816151774256624771)
XLA Ops:
  0.6 0.0 copy-start
  0.6 1.0 %copy-done = f32[2,4,128,128]{3,2,1,0:T(8,128)S(1)} copy-done((f32[2,4,128,128]{3,2,1,0:T(8,128)S(1)}, f32[2,4,128,128]{3,2,1,0:T(8,128)}, u32[]{:S(2)}) %copy-start) | copy-done | bytes 524312
  1.7 0.0 copy-start.1
  1.7 0.9 %copy-done.1 = f32[2,128,128]{2,1,0:T(8,128)S(1)} copy-done((f32[2,128,128]{2,1,0:T(8,128)S(1)}, f32[2,128,128]{2,1,0:T(8,128)}, u32[]{:S(2)}) %copy-start.1) | copy-done | bytes 131096
  2.6 0.0 copy-start.2
  2.6 0.7 %copy-done.2 = f32[2,16,128]{2,1,0:T(8,128)S(1)} copy-done((f32[2,16,128]{2,1,0:T(8,128)S(1)}, f32[2,16,128]{2,1,0:T(8,128)}, u32[]{:S(2)}) %copy-start.2) | copy-done | bytes 16408
  3.3 0.0 copy-start.3
  3.3 0.7 %copy-done.3 = s32[2,4]{1,0:T(2,128)S(1)} copy-done((s32[2,4]{1,0:T(2,128)S(1)}, s32[2,4]{1,0:T(2,128)}, u32[]{:S(2)}) %copy-start.3) | copy-done | bytes 56
  4.0 0.0 copy-start.4
  4.0 0.7 %copy-done.4 = f32[2,128]{1,0:T(2,128)S(1)} copy-done((f32[2,128]{1,0:T(2,128)S(1)}, f32[2,128]{1,0:T(2,128)}, u32[]{:S(2)}) %copy-start.4) | copy-done | bytes 1048
  4.7 0.0 copy-start.5
  4.7 0.7 %copy-done.5 = s32[2]{0:T(128)S(1)} copy-done((s32[2]{0:T(128)S(1)}, s32[2]{0:T(128)}, u32[]{:S(2)}) %copy-start.5) | copy-done | bytes 32
  5.3 47.1 %cg.1 = (f32[2,16,128]{2,1,0:T(8,128)S(1)}, f32[2,16,128]{2,1,0:T(8,128)S(1)}) custom-call(f32[2,16,128]{2,1,0:T(8,128)S(1)} %copy-done.2, f32[2,128,128]{2,1,0:T(8,128)S(1)} %copy-done.1, f32[2,4,128,128]{3,2,1,0:T(8,128)S(1)} %copy-done, s32[2,4]{1,0:T(2,128)S(1)} %copy-done.3, s32[2]{0:T(128)S(1)} %copy-done.5, f32[2,128]{1,0:T(2,128)S(1)} %copy-done.4), custom_call_target="tpu_custom_call" | custom-call | tf_op jit(solution)/shard_map/cg/pallas_call | solution.py:377
  52.4 0.6 %copy.10 = f32[2,16,128]{2,1,0:T(8,128)} copy(f32[2,16,128]{2,1,0:T(8,128)S(1)} %get-tuple-element.4) | data formatting | bytes 32768
  53.0 0.6 %copy.11 = f32[2,16,128]{2,1,0:T(8,128)} copy(f32[2,16,128]{2,1,0:T(8,128)S(1)} %get-tuple-element.5) | data formatting | bytes 32768
Async XLA Ops:
  0.6 1.0 %copy-start = (f32[2,4,128,128]{3,2,1,0:T(8,128)S(1)}, f32[2,4,128,128]{3,2,1,0:T(8,128)}, u32[]{:S(2)}) copy-start(f32[2,4,128,128]{3,2,1,0:T(8,128)} %blocks_ref.1) | copy-start | bytes 1572868
  1.7 0.9 %copy-start.1 = (f32[2,128,128]{2,1,0:T(8,128)S(1)}, f32[2,128,128]{2,1,0:T(8,128)}, u32[]{:S(2)}) copy-start(f32[2,128,128]{2,1,0:T(8,128)} %diag_ref.1) | copy-start | bytes 393220
  2.6 0.7 %copy-start.2 = (f32[2,16,128]{2,1,0:T(8,128)S(1)}, f32[2,16,128]{2,1,0:T(8,128)}, u32[]{:S(2)}) copy-start(f32[2,16,128]{2,1,0:T(8,128)} %right_ref.1) | copy-start | bytes 49156
  3.3 0.7 %copy-start.3 = (s32[2,4]{1,0:T(2,128)S(1)}, s32[2,4]{1,0:T(2,128)}, u32[]{:S(2)}) copy-start(s32[2,4]{1,0:T(2,128)} %cols_ref.1) | copy-start | bytes 100
  4.0 0.7 %copy-start.4 = (f32[2,128]{1,0:T(2,128)S(1)}, f32[2,128]{1,0:T(2,128)}, u32[]{:S(2)}) copy-start(f32[2,128]{1,0:T(2,128)} %celld_ref.1) | copy-start | bytes 3076
  4.7 0.7 %copy-start.5 = (s32[2]{0:T(128)S(1)}, s32[2]{0:T(128)}, u32[]{:S(2)}) copy-start(s32[2]{0:T(128)} %count_ref.1) | copy-start | bytes 28

commit v2 on v1

--- a/solution.py
+++ b/solution.py
@@ -28,11 +28,10 @@
 
 
 def kernel(
-    right_ref, diag_ref, blocks_ref, cols_ref, count_ref, celld_ref,
-    x_out, res_out,
-    rhs, dst, diag_in, dcell, sym, blocks, table_v, table_w, place_s, slot_s, w_off, w_sym,
+    right_ref, diag_ref, blocks_ref, cols_ref, celld_ref, out_ref,
+    rhs, dst, diag_in, dcell, sym, blocks, cols_v, place_s, slot_s, w_off, w_sym,
     mine, win_0, win_1, win_2, prods, spread, tin, red_src, red_a, red_b, outs,
-    local_sems, pair_send, pair_recv, ex_send, ex_recv, red_send, red_recv,
+    local_sems, pair_send, pair_recv, ex_send, ex_recv, red_send, red_recv, meet,
 ):
     dom, sub = lax.axis_index("dom"), lax.axis_index("sub")
     xx, zz = dom // Z, lax.rem(dom, Z)
@@ -56,6 +55,7 @@
         pltpu.make_async_copy(right_ref.at[:, pl.ds(HALF * core, HALF)], rhs.at[own], local_sems.at[1]),
         pltpu.make_async_copy(diag_ref, diag_in, local_sems.at[2]),
         pltpu.make_async_copy(blocks_ref, blocks.at[own], local_sems.at[3]),
+        pltpu.make_async_copy(cols_ref, cols_v.at[core], local_sems.at[4]),
     ]
     for load in loads:
         load.start()
@@ -68,27 +68,49 @@
     barrier = pltpu.get_barrier_semaphore()
     plane = [(dx, dy) for dx in range(X) for dy in range(Y) if dx or dy]
     plane.sort(key=lambda p: -(min(p[0], X - p[0]) + min(p[1], Y - p[1])))
-    greet = [partner]
-    greet += [at(0, 0, dz) for dz in ring_order(Z)]
+    greet = [dom_at(step, dy) for dy in (2, 1, 3, 0) for step in (1, -1)]
+    greet += [at(0, 0, dz) for dz in (1, Z - 1)]
     greet += [at(dx, dy, 0) for dx, dy in plane]
-    greet += [dom_at(step, dy) for step in (1, -1) for dy in range(Y)]
-    for device in greet:
-        pl.semaphore_signal(barrier, inc=1, device_id=device, device_id_type=MESH)
+
+    @pl.when(core == 0)
+    def _():
+        pl.semaphore_signal(barrier, inc=1, device_id=partner, device_id_type=MESH)
+
+    for to_dom, to_sub in greet:
+        pl.semaphore_signal(
+            barrier, inc=1, device_id=(to_dom, to_sub - core), device_id_type=MESH
+        )
+
+    def to_partner(index, source, target):
+        copy = pltpu.make_async_remote_copy(
+            src_ref=source, dst_ref=target, send_sem=pair_send.at[index], recv_sem=pair_recv.at[index],
+            device_id=partner, device_id_type=MESH,
+        )
+        copy.start()
+        return copy
+
+    @pl.when(core == 1)
+    def _():
+        pl.semaphore_wait(barrier, 1)
+        pl.semaphore_signal(meet.at[0], inc=1, device_id=partner, device_id_type=MESH)
+
+    @pl.when(core == 0)
+    def _():
+        pl.semaphore_wait(meet.at[0], 1)
+
+    pair = [
+        to_partner(0, right_ref.at[:, pl.ds(HALF * other, HALF)], rhs.at[own]),
+        to_partner(2, cols_ref, cols_v.at[core]),
+        to_partner(3, blocks_ref, blocks.at[own]),
+    ]
 
     for h in range(4):
         prods[5 * h + K] = jnp.zeros((HALF, BS), F32)
-    lane = lax.broadcasted_iota(I32, (1, BS), 1)
-    places = []
-    for i in range(2):
-        row = jnp.zeros((1, BS), I32)
-        for k in range(K):
-            place = jnp.where(k < count_ref[i], cols_ref[i, k], 2 * GROUP)
-            row = jnp.where(lane == k, place, row)
-            places.append(place)
-        table_v[i : i + 1, :] = row
-    table_v[2:8, :] = jnp.zeros((6, BS), I32)
-
-    def tabulate(base, places):
+    def tabulate(which):
+        base = 2 * which
+        columns = cols_v[which]
+        places = [columns[i, k] for i in range(2) for k in range(K)]
+        places = [jnp.where(place > 0, place, 2 * GROUP) for place in places]
         for i in range(2):
             for k in range(K):
                 place_s[(base + i) * K + k] = places[i * K + k]
@@ -98,34 +120,34 @@
                     slot = jnp.where(places[i * K + k] == w, k, slot)
                 slot_s[(base + i) * 2 * GROUP + w] = slot + (base + i) * (K + 1)
 
-    tabulate(2 * core, places)
+    loads[4].wait()
+    tabulate(core)
 
     loads[0].wait()
     for i in range(2):
         dst[2 * core + i] = jnp.broadcast_to(dcell[i : i + 1, :], (HALF, BS))
+    pair.insert(1, to_partner(1, dst.at[own], dst.at[own]))
     loads[2].wait()
     upper = lax.broadcasted_iota(I32, (BS, BS), 0) < lax.broadcasted_iota(I32, (BS, BS), 1)
     for i in range(2):
         part = jnp.where(upper, diag_in[i], 0.0)
         sym[2 * core + i] = part + part.T
-
-    pl.semaphore_wait(barrier, len(greet))
-
-    def to_partner(index, source, target):
-        copy = pltpu.make_async_remote_copy(
-            src_ref=source, dst_ref=target, send_sem=pair_send.at[index], recv_sem=pair_recv.at[index],
-            device_id=partner, device_id_type=MESH,
-        )
-        copy.start()
-        return copy
-
-    pair = [
-        to_partner(0, right_ref.at[:, pl.ds(HALF * other, HALF)], rhs.at[own]),
-        to_partner(1, dst.at[own], dst.at[own]),
-        to_partner(2, table_v, table_w),
-        to_partner(3, blocks_ref, blocks.at[own]),
-        to_partner(4, sym.at[own], sym.at[own]),
-    ]
+    pair.append(to_partner(4, sym.at[own], sym.at[own]))
+
+    @pl.when(core == 0)
+    def _():
+        pl.semaphore_wait(barrier, 2 * len(greet))
+        pl.semaphore_signal(meet.at[0], inc=1, device_id=partner, device_id_type=MESH)
+
+    @pl.when(core == 1)
+    def _():
+        pl.semaphore_wait(meet.at[0], 1)
+
+    def hail(step, distance):
+        for dz in (distance, Z - distance):
+            pl.semaphore_signal(meet.at[step], inc=1, device_id=at(0, 0, dz), device_id_type=MESH)
+
+    hail(1, 1)
 
     def widen(h):
         for k in range(K):
@@ -238,8 +260,7 @@
         if j == 0:
             loads[3].wait()
             pair[2].wait_recv()
-            rows = table_w[...]
-            tabulate(2 * other, [rows[i, k] for i in range(2) for k in range(K)])
+            tabulate(other)
             pair[3].wait_recv()
             for h in range(4):
                 widen(h)
@@ -271,6 +292,9 @@
                     )
                 )
             )
+        pl.semaphore_wait(meet.at[j + 1], 2)
+        if j < ITERS - 1:
+            hail(j + 2, 2 << j)
         if j == ITERS - 1:
             terms.append(sum(field[h] * (2.0 * ahead[h] + near[h]) for h in range(4)))
         else:
@@ -355,9 +379,9 @@
 
     mine_half = pl.ds(HALF * core, HALF)
     ends = []
-    for i, out in enumerate((x_out, res_out)):
-        ends.append(to_partner(5 + i, outs.at[i, theirs], out.at[:, mine_half]))
-        keep = pltpu.make_async_copy(outs.at[i, own], out.at[:, mine_half], local_sems.at[5 + i])
+    for i in range(2):
+        ends.append(to_partner(5 + i, outs.at[i, theirs], out_ref.at[i, :, mine_half]))
+        keep = pltpu.make_async_copy(outs.at[i, own], out_ref.at[i, :, mine_half], local_sems.at[5 + i])
         keep.start()
         ends.append(keep)
     for j in range(ITERS):
@@ -372,13 +396,11 @@
 
 def local(right_side, diag_blocks, block_values, block_cols, block_count, cell_diagonal):
     hbm = pl.BlockSpec(memory_space=pl.ANY)
-    smem = pl.BlockSpec(memory_space=pltpu.SMEM)
-    shape = jax.ShapeDtypeStruct(right_side.shape, F32)
-    return pl.pallas_call(
+    both = pl.pallas_call(
         kernel,
-        out_shape=(shape, shape),
-        in_specs=[hbm, hbm, hbm, smem, smem, hbm],
-        out_specs=(hbm, hbm),
+        out_shape=jax.ShapeDtypeStruct((2, *right_side.shape), F32),
+        in_specs=[hbm] * 5,
+        out_specs=hbm,
         scratch_shapes=[
             pltpu.VMEM((4, HALF, BS), F32),
             pltpu.VMEM((4, HALF, BS), F32),
@@ -386,8 +408,7 @@
             pltpu.VMEM((2, BS), F32),
             pltpu.VMEM((4, BS, BS), F32),
             pltpu.VMEM((4, K, BS, BS), F32),
-            pltpu.VMEM((8, BS), I32),
-            pltpu.VMEM((8, BS), I32),
+            pltpu.VMEM((2, 2, K), I32),
             pltpu.SMEM((4 * K,), I32),
             pltpu.SMEM((4 * 2 * GROUP,), I32),
             pltpu.VMEM((4, 2 * BS, K * BS), BF16),
@@ -410,12 +431,14 @@
             pltpu.SemaphoreType.DMA((ITERS, 4)),
             pltpu.SemaphoreType.DMA((2,)),
             pltpu.SemaphoreType.DMA((2,)),
+            pltpu.SemaphoreType.REGULAR((4,)),
         ],
         compiler_params=pltpu.CompilerParams(
-            collective_id=0, has_side_effects=True, vmem_limit_bytes=24 << 20
+            collective_id=0, has_side_effects=True, vmem_limit_bytes=60 << 20
         ),
         name="cg",
-    )(right_side, diag_blocks, block_values, block_cols, block_count, cell_diagonal)
+    )(right_side, diag_blocks, block_values, block_cols, cell_diagonal)
+    return both[0], both[1]
 
 
 def solution(mesh):

time: 53.9 us -> 46.7 us (0.87)
  local copies, waits for them, and re-layouts: 5.88 us -> 1.35 us
  Pallas kernels: 47.1 us -> 44.5 us
    unnamed x14 -> x0, local copies, waits for them, and re-layouts: 5.88 us -> none
    pallas_call x1, Pallas kernels: 47.1 us -> 44.5 us  [local(): pl.pallas_call(kernel, out_shape=jax.ShapeDtypeStruct((2, *right_side.sha...]
    squeeze x0 -> x1, local copies, waits for them, and re-layouts: none -> 1.35 us  [local(): return (both[0], both[1])]
where the time goes in v2:
time: 46.7 us; the launch traced here: 46.5 us
  Pallas kernels  44.5 us (95%)
  local copies, waits for them, and re-layouts  1.35 us (3%)
  between operations  0.64 us (1%)
    pallas_call x1, Pallas kernels, local(): pl.pallas_call(kernel, out_shape=jax.ShapeDtypeStruct((2, *right_side.sha...  44.5 us
    squeeze x1, local copies, waits for them, and re-layouts, local(): return (both[0], both[1])  1.35 us

profile of v2, /device:TPU:1, one launch (start us, length us, event | category | flops | bytes accessed | tf_op | source)
XLA Modules:
  0.0 46.5 jit_solution(11467592044914871866)
XLA Ops:
  0.6 44.5 %cg.1 = f32[2,2,16,128]{3,2,1,0:T(8,128)} custom-call(f32[2,16,128]{2,1,0:T(8,128)} %right_ref.1, f32[2,128,128]{2,1,0:T(8,128)} %diag_ref.1, f32[2,4,128,128]{3,2,1,0:T(8,128)} %blocks_ref.1, s32[2,4]{1,0:T(2,128)} %cols_ref.1, f32[2,128]{1,0:T(2,128)} %celld_ref.1), custom_call_target="tpu_custom_call" | custom-call | tf_op jit(solution)/shard_map/cg/pallas_call | solution.py:399
  45.2 1.3 %slice_bitcast_fusion = (f32[2,16,128]{2,1,0:T(8,128)}, f32[2,16,128]{2,1,0:T(8,128)}) fusion(f32[2,2,16,128]{3,2,1,0:T(8,128)} %cg.1), kind=kLoop, calls=%fused_computation | loop fusion | bytes 65536 | tf_op jit(solution)/shard_map/squeeze | solution.py:441

commit v3 on v2

--- a/solution.py
+++ b/solution.py
@@ -69,7 +69,7 @@
     plane = [(dx, dy) for dx in range(X) for dy in range(Y) if dx or dy]
     plane.sort(key=lambda p: -(min(p[0], X - p[0]) + min(p[1], Y - p[1])))
     greet = [dom_at(step, dy) for dy in (2, 1, 3, 0) for step in (1, -1)]
-    greet += [at(0, 0, dz) for dz in (1, Z - 1)]
+    greet += [at(0, 0, dz) for dz in (1, 2, Z - 2, Z - 1)]
     greet += [at(dx, dy, 0) for dx, dy in plane]
 
     @pl.when(core == 0)
@@ -143,11 +143,13 @@
     def _():
         pl.semaphore_wait(meet.at[0], 1)
 
-    def hail(step, distance):
-        for dz in (distance, Z - distance):
-            pl.semaphore_signal(meet.at[step], inc=1, device_id=at(0, 0, dz), device_id_type=MESH)
-
-    hail(1, 1)
+    reach = ((1, 2, Z - 2, Z - 1), (4, Z - 4), (6, Z - 6))
+
+    def hail(step):
+        for dz in reach[step]:
+            pl.semaphore_signal(meet.at[step + 1], inc=1, device_id=at(0, 0, dz), device_id_type=MESH)
+
+    hail(0)
 
     def widen(h):
         for k in range(K):
@@ -177,12 +179,13 @@
     def await_bytes(sem, buffer):
         pltpu.make_async_copy(buffer, buffer, sem).wait()
 
-    def send_field(j):
+    def send_field_back(j, order):
         @pl.when(dom > 0)
         def _():
-            for dy in (2, 1, 3, 0):
+            for dy in order:
                 exchange(0, j, mine.at[j], win[j].at[pl.ds(GROUP + 4 * yy, 4)], dom_at(-1, dy)).start()
 
+    def send_field_own(j):
         for y_here in range(1, Y):
             @pl.when(yy == y_here)
             def _():
@@ -191,13 +194,14 @@
                         1, j, mine.at[j], win[j].at[pl.ds(4 * y_here, 4)], (dom, 2 * y_there + core)
                     ).start()
 
-    def send_products(j):
+    def send_products_on(j, order):
         @pl.when(dom < N_DOM - 1)
         def _():
-            for dy in (2, 1, 3, 0):
+            for dy in order:
                 rows = pl.ds(GROUP + 4 * lax.rem(yy + dy, Y), 4)
                 exchange(2, j, spread.at[j, rows], tin.at[j, Y + yy], dom_at(1, dy)).start()
 
+    def send_products_own(j):
         for y_here in range(Y - 1):
             @pl.when(yy == y_here)
             def _():
@@ -255,7 +259,7 @@
         for h in range(4):
             mine[j, h] = field[h]
             win[j][4 * yy + h] = field[h]
-        send_field(j)
+        send_field_back(j, (2,))
         parts = [split(field[h]) for h in range(4)]
         if j == 0:
             loads[3].wait()
@@ -270,10 +274,21 @@
             )
             for k in range(K):
                 prods[5 * h + k] = out[0:HALF, k * BS : (k + 1) * BS] + out[HALF:, k * BS : (k + 1) * BS]
-        for w in range(2 * GROUP):
-            picked = [prods[slot_s[h * 2 * GROUP + w]] for h in range(4)]
-            spread[j, w] = (picked[0] + picked[1]) + (picked[2] + picked[3])
-        send_products(j)
+
+        def gather_products(first):
+            for w in range(first, first + GROUP):
+                picked = [prods[slot_s[h * 2 * GROUP + w]] for h in range(4)]
+                spread[j, w] = (picked[0] + picked[1]) + (picked[2] + picked[3])
+
+        gather_products(GROUP)
+        send_products_on(j, (2,))
+        send_field_back(j, (1, 3))
+        send_products_on(j, (1, 3))
+        send_field_own(j)
+        gather_products(0)
+        send_products_own(j)
+        send_field_back(j, (0,))
+        send_products_on(j, (0,))
         if j == 0:
             pair[4].wait_recv()
             for h in range(4):
@@ -281,7 +296,13 @@
         near = [
             fold(lax.dot_general(parts[h], w_sym[h], across, preferred_element_type=F32)) for h in range(4)
         ]
-        await_field(j)
+        if j == ITERS - 1:
+            await_field(j)
+            pl.semaphore_wait(meet.at[j + 1], len(reach[j]))
+        else:
+            pl.semaphore_wait(meet.at[j + 1], len(reach[j]))
+            hail(j + 1)
+            await_field(j)
         ahead = []
         for h in range(4):
             tiles = [split(win[j][place_s[h * K + k]]) for k in range(K)]
@@ -292,9 +313,6 @@
                     )
                 )
             )
-        pl.semaphore_wait(meet.at[j + 1], 2)
-        if j < ITERS - 1:
-            hail(j + 2, 2 << j)
         if j == ITERS - 1:
             terms.append(sum(field[h] * (2.0 * ahead[h] + near[h]) for h in range(4)))
         else:
@@ -311,27 +329,28 @@
             terms.append(sum(u[j + 1][h] * applied[h] for h in range(4)))
 
     lanes = lax.broadcasted_iota(I32, (HALF, BS), 1)
-    tile = jnp.zeros((HALF, BS), F32)
+    sides = lax.broadcasted_iota(I32, (HALF, BS), 0)
+    row = jnp.zeros((HALF, BS), F32)
     for index, term in enumerate(terms):
-        tile = jnp.where(lanes == index, jnp.sum(term, axis=1, keepdims=True), tile)
-
-    def reduced(stage, buffer, slot, devices, tile):
-        red_src[stage] = tile
-        buffer[slot] = tile
-        for device in devices:
-            pltpu.make_async_remote_copy(
-                src_ref=red_src.at[stage], dst_ref=buffer.at[slot], send_sem=red_send.at[stage],
-                recv_sem=red_recv.at[stage], device_id=device, device_id_type=MESH,
-            ).start()
-
-    def total(stage, buffer, count):
-        await_bytes(red_recv.at[stage], buffer.at[pl.ds(0, count - 1)])
-        values = [buffer[i] for i in range(count)]
-        while len(values) > 1:
-            values = [values[i] + values[i + 1] for i in range(0, len(values), 2)]
-        return values[0]
-
-    reduced(0, red_a, Y * xx + yy, [at(dx, dy, 0) for dx, dy in plane], tile)
+        row = jnp.where(lanes == HALF * index + sides, jnp.sum(term, axis=1, keepdims=True), row)
+    row = jnp.sum(row, axis=0, keepdims=True)
+    chip = (Y * xx + yy) * Z + zz
+    red_a[chip] = row
+    red_src[0] = row
+
+    def send_row(source, target, stage, device):
+        pltpu.make_async_remote_copy(
+            src_ref=source, dst_ref=target, send_sem=red_send.at[stage], recv_sem=red_recv.at[stage],
+            device_id=device, device_id_type=MESH,
+        ).start()
+
+    for dx, dy in plane:
+        send_row(red_src.at[0], red_a.at[chip], 0, at(dx, dy, Z - zz))
+
+    @pl.when(zz > 0)
+    def _():
+        send_row(red_src.at[0], red_a.at[chip], 0, at(0, 0, Z - zz))
+
     last = ITERS - 1
     await_products(last)
     applied = []
@@ -341,11 +360,29 @@
             back = back + tin[last, s, h]
         applied.append(near[h] + ahead[h] + back)
     image.append(applied)
-    tile = total(0, red_a, X * Y)
-    reduced(1, red_b, zz, [at(0, 0, dz) for dz in ring_order(Z)], tile)
-    tile = total(1, red_b, Z)
-
-    gram = [jnp.broadcast_to(tile[:, i : i + 1], (HALF, BS)) for i in range(2 * ITERS)]
+
+    @pl.when(zz == 0)
+    def _():
+        await_bytes(red_recv.at[0], red_a.at[pl.ds(0, X * Y * Z - 1)])
+        values = [red_a[i] for i in range(X * Y * Z)]
+        while len(values) > 1:
+            values = [values[i] + values[i + 1] for i in range(0, len(values), 2)]
+        red_b[0] = values[0]
+        red_src[1] = values[0]
+        for dz in range(1, Z):
+            send_row(red_src.at[1], red_b.at[0], 1, at(0, 0, dz))
+
+    @pl.when(zz > 0)
+    def _():
+        await_bytes(red_recv.at[1], red_b)
+
+    row = red_b[0]
+    gram = [
+        jnp.broadcast_to(
+            jnp.sum(jnp.where(lanes == HALF * i + sides, row, 0.0), axis=1, keepdims=True), (HALF, BS)
+        )
+        for i in range(2 * ITERS)
+    ]
 
     def inner(a, b):
         value = None
@@ -387,7 +424,15 @@
     for j in range(ITERS):
         await_sends(j)
     await_bytes(red_send.at[0], red_a.at[pl.ds(0, X * Y - 1)])
-    await_bytes(red_send.at[1], red_b.at[pl.ds(0, Z - 1)])
+
+    @pl.when(zz > 0)
+    def _():
+        await_bytes(red_send.at[0], red_b)
+
+    @pl.when(zz == 0)
+    def _():
+        await_bytes(red_send.at[1], red_a.at[pl.ds(0, Z - 1)])
+
     for copy in pair:
         copy.wait_send()
     for copy in ends:
@@ -420,9 +465,9 @@
             pltpu.VMEM((4 * (K + 1), HALF, BS), F32),
             pltpu.VMEM((ITERS, 2 * GROUP, HALF, BS), F32),
             pltpu.VMEM((ITERS, 2 * Y, 4, HALF, BS), F32),
-            pltpu.VMEM((2, HALF, BS), F32),
-            pltpu.VMEM((X * Y, HALF, BS), F32),
-            pltpu.VMEM((Z, HALF, BS), F32),
+            pltpu.VMEM((2, 1, BS), F32),
+            pltpu.VMEM((X * Y * Z, 1, BS), F32),
+            pltpu.VMEM((1, 1, BS), F32),
             pltpu.VMEM((2, 4, HALF, BS), F32),
             pltpu.SemaphoreType.DMA((7,)),
             pltpu.SemaphoreType.DMA((7,)),

time: 46.7 us -> 45.2 us (0.968)
  the two profiles are of different devices: /device:TPU:1 before, /device:TPU:33 now
where the time goes in v3:
time: 45.2 us; the launch traced here: 45 us
  Pallas kernels  43 us (95%)
  local copies, waits for them, and re-layouts  1.35 us (3%)
  between operations  0.64 us (1%)
    pallas_call x1, Pallas kernels, local(): pl.pallas_call(kernel, out_shape=jax.ShapeDtypeStruct((2, *right_side.sha...  43 us
    squeeze x1, local copies, waits for them, and re-layouts, local(): return (both[0], both[1])  1.35 us

profile of v3, /device:TPU:33, one launch (start us, length us, event | category | flops | bytes accessed | tf_op | source)
XLA Modules:
  0.0 45.0 jit_solution(9671708925339403731)
XLA Ops:
  0.6 43.0 %cg.1 = f32[2,2,16,128]{3,2,1,0:T(8,128)} custom-call(f32[2,16,128]{2,1,0:T(8,128)} %right_ref.1, f32[2,128,128]{2,1,0:T(8,128)} %diag_ref.1, f32[2,4,128,128]{3,2,1,0:T(8,128)} %blocks_ref.1, s32[2,4]{1,0:T(2,128)} %cols_ref.1, f32[2,128]{1,0:T(2,128)} %celld_ref.1), custom_call_target="tpu_custom_call" | custom-call | tf_op jit(solution)/shard_map/cg/pallas_call | solution.py:444
  43.6 1.3 %slice_bitcast_fusion = (f32[2,16,128]{2,1,0:T(8,128)}, f32[2,16,128]{2,1,0:T(8,128)}) fusion(f32[2,2,16,128]{3,2,1,0:T(8,128)} %cg.1), kind=kLoop, calls=%fused_computation | loop fusion | bytes 65536 | tf_op jit(solution)/shard_map/squeeze | solution.py:486

commit v4 on v3

--- a/solution.py
+++ b/solution.py
@@ -123,6 +123,18 @@
     loads[4].wait()
     tabulate(core)
 
+    def widen(h):
+        for k in range(K):
+            block = blocks[h, k]
+            high = block.astype(BF16)
+            w_off[h, 0:BS, k * BS : (k + 1) * BS] = high
+            w_off[h, BS : 2 * BS, k * BS : (k + 1) * BS] = (block - high.astype(F32)).astype(BF16)
+
+    def widen_sym(h):
+        high = sym[h].astype(BF16)
+        w_sym[h, 0:BS, :] = high
+        w_sym[h, BS : 2 * BS, :] = (sym[h] - high.astype(F32)).astype(BF16)
+
     loads[0].wait()
     for i in range(2):
         dst[2 * core + i] = jnp.broadcast_to(dcell[i : i + 1, :], (HALF, BS))
@@ -133,6 +145,11 @@
         part = jnp.where(upper, diag_in[i], 0.0)
         sym[2 * core + i] = part + part.T
     pair.append(to_partner(4, sym.at[own], sym.at[own]))
+    loads[3].wait()
+    for i in range(2):
+        widen(2 * core + i)
+    pair[2].wait_recv()
+    tabulate(other)
 
     @pl.when(core == 0)
     def _():
@@ -150,18 +167,6 @@
             pl.semaphore_signal(meet.at[step + 1], inc=1, device_id=at(0, 0, dz), device_id_type=MESH)
 
     hail(0)
-
-    def widen(h):
-        for k in range(K):
-            block = blocks[h, k]
-            high = block.astype(BF16)
-            w_off[h, 0:BS, k * BS : (k + 1) * BS] = high
-            w_off[h, BS : 2 * BS, k * BS : (k + 1) * BS] = (block - high.astype(F32)).astype(BF16)
-
-    def widen_sym(h):
-        high = sym[h].astype(BF16)
-        w_sym[h, 0:BS, :] = high
-        w_sym[h, BS : 2 * BS, :] = (sym[h] - high.astype(F32)).astype(BF16)
 
     loads[1].wait()
     pair[0].wait_recv()
@@ -250,6 +255,16 @@
     def fold(out):
         return (out[0:HALF, 0:BS] + out[0:HALF, BS:]) + (out[HALF:, 0:BS] + out[HALF:, BS:])
 
+    lanes = lax.broadcasted_iota(I32, (HALF, BS), 1)
+    sides = lax.broadcasted_iota(I32, (HALF, BS), 0)
+
+    def in_row(first, terms):
+        values = jnp.zeros((HALF, BS), F32)
+        for index, term in enumerate(terms):
+            place = HALF * (first + index) + sides
+            values = jnp.where(lanes == place, jnp.sum(term, axis=1, keepdims=True), values)
+        return values
+
     across = (((1,), (1,)), ((), ()))
     terms = []
     terms.append(sum(rhs[h] * u[0][h] for h in range(4)))
@@ -262,12 +277,9 @@
         send_field_back(j, (2,))
         parts = [split(field[h]) for h in range(4)]
         if j == 0:
-            loads[3].wait()
-            pair[2].wait_recv()
-            tabulate(other)
             pair[3].wait_recv()
-            for h in range(4):
-                widen(h)
+            for i in range(2):
+                widen(2 * other + i)
         for h in range(4):
             out = jnp.dot(
                 jnp.concatenate([parts[h], parts[h]], axis=1), w_off[h], preferred_element_type=F32
@@ -297,6 +309,7 @@
             fold(lax.dot_general(parts[h], w_sym[h], across, preferred_element_type=F32)) for h in range(4)
         ]
         if j == ITERS - 1:
+            row = in_row(0, terms)
             await_field(j)
             pl.semaphore_wait(meet.at[j + 1], len(reach[j]))
         else:
@@ -328,12 +341,7 @@
             terms.append(sum(field[h] * applied[h] for h in range(4)))
             terms.append(sum(u[j + 1][h] * applied[h] for h in range(4)))
 
-    lanes = lax.broadcasted_iota(I32, (HALF, BS), 1)
-    sides = lax.broadcasted_iota(I32, (HALF, BS), 0)
-    row = jnp.zeros((HALF, BS), F32)
-    for index, term in enumerate(terms):
-        row = jnp.where(lanes == HALF * index + sides, jnp.sum(term, axis=1, keepdims=True), row)
-    row = jnp.sum(row, axis=0, keepdims=True)
+    row = jnp.sum(row + in_row(2 * ITERS - 1, terms[2 * ITERS - 1 :]), axis=0, keepdims=True)
     chip = (Y * xx + yy) * Z + zz
     red_a[chip] = row
     red_src[0] = row
@@ -344,12 +352,13 @@
             device_id=device, device_id_type=MESH,
         ).start()
 
-    for dx, dy in plane:
-        send_row(red_src.at[0], red_a.at[chip], 0, at(dx, dy, Z - zz))
-
-    @pl.when(zz > 0)
-    def _():
-        send_row(red_src.at[0], red_a.at[chip], 0, at(0, 0, Z - zz))
+    for z_root in range(2):
+        for dx, dy in plane:
+            send_row(red_src.at[0], red_a.at[chip], 0, at(dx, dy, Z + z_root - zz))
+
+        @pl.when(zz != z_root)
+        def _():
+            send_row(red_src.at[0], red_a.at[chip], 0, at(0, 0, Z + z_root - zz))
 
     last = ITERS - 1
     await_products(last)
@@ -361,7 +370,7 @@
         applied.append(near[h] + ahead[h] + back)
     image.append(applied)
 
-    @pl.when(zz == 0)
+    @pl.when(zz < 2)
     def _():
         await_bytes(red_recv.at[0], red_a.at[pl.ds(0, X * Y * Z - 1)])
         values = [red_a[i] for i in range(X * Y * Z)]
@@ -369,10 +378,18 @@
             values = [values[i] + values[i + 1] for i in range(0, len(values), 2)]
         red_b[0] = values[0]
         red_src[1] = values[0]
-        for dz in range(1, Z):
+
+    @pl.when(zz == 1)
+    def _():
+        for dz in range(1, 8):
             send_row(red_src.at[1], red_b.at[0], 1, at(0, 0, dz))
 
-    @pl.when(zz > 0)
+    @pl.when(zz == 0)
+    def _():
+        for dz in range(9, 16):
+            send_row(red_src.at[1], red_b.at[0], 1, at(0, 0, dz))
+
+    @pl.when(zz > 1)
     def _():
         await_bytes(red_recv.at[1], red_b)
 
@@ -423,15 +440,15 @@
         ends.append(keep)
     for j in range(ITERS):
         await_sends(j)
-    await_bytes(red_send.at[0], red_a.at[pl.ds(0, X * Y - 1)])
-
-    @pl.when(zz > 0)
+    await_bytes(red_send.at[0], red_a.at[pl.ds(0, 2 * X * Y - 1)])
+
+    @pl.when(zz > 1)
     def _():
         await_bytes(red_send.at[0], red_b)
 
-    @pl.when(zz == 0)
-    def _():
-        await_bytes(red_send.at[1], red_a.at[pl.ds(0, Z - 1)])
+    @pl.when(zz < 2)
+    def _():
+        await_bytes(red_send.at[1], red_a.at[pl.ds(0, 7)])
 
     for copy in pair:
         copy.wait_send()

time: 45.2 us -> 44.7 us (0.989)
  the two profiles are of different devices: /device:TPU:33 before, /device:TPU:1 now
where the time goes in v4:
time: 44.7 us; the launch traced here: 44.5 us
  Pallas kernels  42.5 us (95%)
  local copies, waits for them, and re-layouts  1.35 us (3%)
  between operations  0.64 us (1%)
    pallas_call x1, Pallas kernels, local(): pl.pallas_call(kernel, out_shape=jax.ShapeDtypeStruct((2, *right_side.sha...  42.5 us
    squeeze x1, local copies, waits for them, and re-layouts, local(): return (both[0], both[1])  1.35 us

profile of v4, /device:TPU:1, one launch (start us, length us, event | category | flops | bytes accessed | tf_op | source)
XLA Modules:
  0.0 44.5 jit_solution(3456215036324188588)
XLA Ops:
  0.6 42.5 %cg.1 = f32[2,2,16,128]{3,2,1,0:T(8,128)} custom-call(f32[2,16,128]{2,1,0:T(8,128)} %right_ref.1, f32[2,128,128]{2,1,0:T(8,128)} %diag_ref.1, f32[2,4,128,128]{3,2,1,0:T(8,128)} %blocks_ref.1, s32[2,4]{1,0:T(2,128)} %cols_ref.1, f32[2,128]{1,0:T(2,128)} %celld_ref.1), custom_call_target="tpu_custom_call" | custom-call | tf_op jit(solution)/shard_map/cg/pallas_call | solution.py:461
  43.1 1.3 %slice_bitcast_fusion = (f32[2,16,128]{2,1,0:T(8,128)}, f32[2,16,128]{2,1,0:T(8,128)}) fusion(f32[2,2,16,128]{3,2,1,0:T(8,128)} %cg.1), kind=kLoop, calls=%fused_computation | loop fusion | bytes 65536 | tf_op jit(solution)/shard_map/squeeze | solution.py:503

commit v5 on v4

--- a/solution.py
+++ b/solution.py
@@ -15,6 +15,8 @@
 X, Y, Z = 4, 4, 16
 N_DOM = X * Z
 GROUP = 4 * Y
+SIDE = 64
+FAR = range(6, 11)
 F32, BF16, I32 = jnp.float32, jnp.bfloat16, jnp.int32
 
 
@@ -29,8 +31,8 @@
 
 def kernel(
     right_ref, diag_ref, blocks_ref, cols_ref, celld_ref, out_ref,
-    rhs, dst, diag_in, dcell, sym, blocks, cols_v, place_s, slot_s, w_off, w_sym,
-    mine, win_0, win_1, win_2, prods, spread, tin, red_src, red_a, red_b, outs,
+    rhs, rhs_all, image, image_in, dst, diag_in, dcell, sym, blocks, cols_v, place_s, slot_s, w_off, w_sym,
+    mine, win_0, win_1, win_2, prods, spread, tin, red_src, red_a, red_b, red_c, outs,
     local_sems, pair_send, pair_recv, ex_send, ex_recv, red_send, red_recv, meet,
 ):
     dom, sub = lax.axis_index("dom"), lax.axis_index("sub")
@@ -57,6 +59,7 @@
         pltpu.make_async_copy(blocks_ref, blocks.at[own], local_sems.at[3]),
         pltpu.make_async_copy(cols_ref, cols_v.at[core], local_sems.at[4]),
     ]
+    loads.append(pltpu.make_async_copy(right_ref, rhs_all, local_sems.at[5]))
     for load in loads:
         load.start()
 
@@ -173,7 +176,6 @@
     pair[1].wait_recv()
     inverse = [1.0 / dst[h] for h in range(4)]
     u = [[rhs[h] * inverse[h] for h in range(4)]]
-    image = []
 
     def exchange(index, j, source, target, device):
         return pltpu.make_async_remote_copy(
@@ -261,9 +263,14 @@
     def in_row(first, terms):
         values = jnp.zeros((HALF, BS), F32)
         for index, term in enumerate(terms):
-            place = HALF * (first + index) + sides
+            place = SIDE * core + HALF * (first + index) + sides
             values = jnp.where(lanes == place, jnp.sum(term, axis=1, keepdims=True), values)
         return values
+
+    def swap_image(j, applied):
+        for h in range(4):
+            image[j, h] = applied[h]
+        pair.append(to_partner(5 + j, image.at[j, theirs], image_in.at[j]))
 
     across = (((1,), (1,)), ((), ()))
     terms = []
@@ -274,7 +281,9 @@
         for h in range(4):
             mine[j, h] = field[h]
             win[j][4 * yy + h] = field[h]
-        send_field_back(j, (2,))
+        send_field_back(j, (2, 1, 3))
+        send_field_own(j)
+        send_field_back(j, (0,))
         parts = [split(field[h]) for h in range(4)]
         if j == 0:
             pair[3].wait_recv()
@@ -293,13 +302,9 @@
                 spread[j, w] = (picked[0] + picked[1]) + (picked[2] + picked[3])
 
         gather_products(GROUP)
-        send_products_on(j, (2,))
-        send_field_back(j, (1, 3))
-        send_products_on(j, (1, 3))
-        send_field_own(j)
+        send_products_on(j, (2, 1, 3))
         gather_products(0)
         send_products_own(j)
-        send_field_back(j, (0,))
         send_products_on(j, (0,))
         if j == 0:
             pair[4].wait_recv()
@@ -336,29 +341,40 @@
                 for s in range(2 * Y):
                     back = back + tin[j, s, h]
                 applied.append(near[h] + ahead[h] + back)
-            image.append(applied)
+            swap_image(j, applied)
             u.append([applied[h] * inverse[h] for h in range(4)])
             terms.append(sum(field[h] * applied[h] for h in range(4)))
             terms.append(sum(u[j + 1][h] * applied[h] for h in range(4)))
 
     row = jnp.sum(row + in_row(2 * ITERS - 1, terms[2 * ITERS - 1 :]), axis=0, keepdims=True)
-    chip = (Y * xx + yy) * Z + zz
-    red_a[chip] = row
+    slot = (zz * Y * X + Y * xx + yy) * 2 + core
+    red_a[slot] = row
     red_src[0] = row
 
-    def send_row(source, target, stage, device):
+    def send_row(source, target, stage, arrival, device):
         pltpu.make_async_remote_copy(
-            src_ref=source, dst_ref=target, send_sem=red_send.at[stage], recv_sem=red_recv.at[stage],
+            src_ref=source, dst_ref=target, send_sem=red_send.at[stage], recv_sem=red_recv.at[arrival],
             device_id=device, device_id_type=MESH,
         ).start()
 
-    for z_root in range(2):
-        for dx, dy in plane:
-            send_row(red_src.at[0], red_a.at[chip], 0, at(dx, dy, Z + z_root - zz))
-
-        @pl.when(zz != z_root)
-        def _():
-            send_row(red_src.at[0], red_a.at[chip], 0, at(0, 0, Z + z_root - zz))
+    arrival = jnp.where((zz >= FAR[0]) & (zz <= FAR[-1]), 1, 0)
+    for dx, dy in plane:
+        to_dom, to_sub = at(dx, dy, Z - zz)
+        for to in (to_sub, to_sub + 1 - 2 * core):
+            send_row(red_src.at[0], red_a.at[slot], 0, arrival, (to_dom, to))
+    to_dom, to_sub = at(0, 0, Z - zz)
+    send_row(red_src.at[0], red_a.at[slot], 0, arrival, (to_dom, to_sub + 1 - 2 * core))
+
+    @pl.when(zz > 0)
+    def _():
+        send_row(red_src.at[0], red_a.at[slot], 0, arrival, (to_dom, to_sub))
+
+    for dx, dy in plane:
+        send_row(red_src.at[0], red_a.at[slot], 0, arrival, at(dx, dy, Z + 1 - zz))
+
+    @pl.when(zz != 1)
+    def _():
+        send_row(red_src.at[0], red_a.at[slot], 0, arrival, at(0, 0, Z + 1 - zz))
 
     last = ITERS - 1
     await_products(last)
@@ -368,35 +384,60 @@
         for s in range(2 * Y):
             back = back + tin[last, s, h]
         applied.append(near[h] + ahead[h] + back)
-    image.append(applied)
-
-    @pl.when(zz < 2)
-    def _():
-        await_bytes(red_recv.at[0], red_a.at[pl.ds(0, X * Y * Z - 1)])
-        values = [red_a[i] for i in range(X * Y * Z)]
+    swap_image(ITERS - 1, applied)
+
+    near_planes = [z for z in range(Z) if z not in FAR]
+
+    def add_rows(planes, places):
+        values = [red_a[2 * X * Y * z + i] for z in planes for i in places]
         while len(values) > 1:
-            values = [values[i] + values[i + 1] for i in range(0, len(values), 2)]
-        red_b[0] = values[0]
-        red_src[1] = values[0]
+            values = [sum(values[i : i + 2]) for i in range(0, len(values), 2)]
+        return values[0]
+
+    @pl.when(zz == 0)
+    def _():
+        await_bytes(red_recv.at[0], red_a.at[pl.ds(0, 2 * X * Y * len(near_planes) - 1)])
+        near_sum = add_rows(near_planes, range(2 * X * Y))
+        await_bytes(red_recv.at[1], red_a.at[pl.ds(0, 2 * X * Y * len(FAR))])
+        whole = near_sum + add_rows(FAR, range(2 * X * Y))
+        red_b[0] = whole
+        red_src[1] = whole
+        for dz in (2, *range(9, Z)):
+            send_row(red_src.at[1], red_b.at[0], 1, 2, at(0, 0, dz))
 
     @pl.when(zz == 1)
     def _():
-        for dz in range(1, 8):
-            send_row(red_src.at[1], red_b.at[0], 1, at(0, 0, dz))
-
-    @pl.when(zz == 0)
-    def _():
-        for dz in range(9, 16):
-            send_row(red_src.at[1], red_b.at[0], 1, at(0, 0, dz))
+        places = [2 * i + core for i in range(X * Y)]
+        await_bytes(red_recv.at[0], red_a.at[pl.ds(0, X * Y * len(near_planes) - 1)])
+        near_sum = add_rows(near_planes, places)
+        await_bytes(red_recv.at[1], red_a.at[pl.ds(0, X * Y * len(FAR))])
+        whole = near_sum + add_rows(FAR, places)
+        red_src[1] = whole
+        swap = pltpu.make_async_remote_copy(
+            src_ref=red_src.at[1], dst_ref=red_c.at[0], send_sem=red_send.at[2], recv_sem=red_recv.at[3],
+            device_id=partner, device_id_type=MESH,
+        )
+        swap.start()
+        swap.wait_recv()
+        whole = whole + red_c[0]
+        red_b[0] = whole
+        red_src[2] = whole
+        for dz in range(2, 8):
+            send_row(red_src.at[2], red_b.at[0], 1, 2, at(0, 0, dz))
+        swap.wait_send()
 
     @pl.when(zz > 1)
     def _():
-        await_bytes(red_recv.at[1], red_b)
+        await_bytes(red_recv.at[2], red_b)
 
     row = red_b[0]
+    lanes = lax.broadcasted_iota(I32, (2 * HALF, BS), 1)
+    sides = lax.broadcasted_iota(I32, (2 * HALF, BS), 0)
+    first_lane = jnp.where(sides < HALF, SIDE * core + sides, SIDE * other + sides - HALF)
     gram = [
         jnp.broadcast_to(
-            jnp.sum(jnp.where(lanes == HALF * i + sides, row, 0.0), axis=1, keepdims=True), (HALF, BS)
+            jnp.sum(jnp.where(lanes == first_lane + HALF * i, row, 0.0), axis=1, keepdims=True),
+            (2 * HALF, BS),
         )
         for i in range(2 * ITERS)
     ]
@@ -413,7 +454,7 @@
     def plus(a, b):
         return a if b is None else b if a is None else a + b
 
-    one = jnp.ones((HALF, BS), F32)
+    one = jnp.ones((2 * HALF, BS), F32)
     zc, pc, xc = [one, None, None, None], [one, None, None], [None, None, None]
     rho = gram[0]
     for step in range(ITERS):
@@ -427,33 +468,44 @@
             pc = [plus(zc[i], None if pc[i] is None else beta * pc[i]) for i in range(3)]
             rho = fresh
 
-    for h in range(4):
-        outs[0, h] = xc[0] * u[0][h] + xc[1] * u[1][h] + xc[2] * u[2][h]
-        outs[1, h] = zc[0] * rhs[h] + zc[1] * image[0][h] + zc[2] * image[1][h] + zc[3] * image[2][h]
-
-    mine_half = pl.ds(HALF * core, HALF)
-    ends = []
+    loads[5].wait()
+    for copy in pair[5:]:
+        copy.wait_recv()
+    mine_half, their_half = pl.ds(HALF * core, HALF), pl.ds(HALF * other, HALF)
     for i in range(2):
-        ends.append(to_partner(5 + i, outs.at[i, theirs], out_ref.at[i, :, mine_half]))
-        keep = pltpu.make_async_copy(outs.at[i, own], out_ref.at[i, :, mine_half], local_sems.at[5 + i])
-        keep.start()
-        ends.append(keep)
+        h = 2 * core + i
+        x, z = [c[:HALF] for c in xc], [c[:HALF] for c in zc]
+        outs[0, i, mine_half, :] = x[0] * mine[0, h] + x[1] * mine[1, h] + x[2] * mine[2, h]
+        outs[1, i, mine_half, :] = z[0] * rhs[h] + z[1] * image[0, h] + z[2] * image[1, h] + z[3] * image[2, h]
+        x, z = [c[HALF:] for c in xc], [c[HALF:] for c in zc]
+        right, back = rhs_all[i, their_half, :], 1.0 / dst[h]
+        outs[0, i, their_half, :] = (
+            x[0] * (right * back) + x[1] * (image_in[0, i] * back) + x[2] * (image_in[1, i] * back)
+        )
+        outs[1, i, their_half, :] = (
+            z[0] * right + z[1] * image_in[0, i] + z[2] * image_in[1, i] + z[3] * image_in[2, i]
+        )
+    keep = pltpu.make_async_copy(outs, out_ref, local_sems.at[6])
+    keep.start()
     for j in range(ITERS):
         await_sends(j)
-    await_bytes(red_send.at[0], red_a.at[pl.ds(0, 2 * X * Y - 1)])
+    await_bytes(red_send.at[0], red_a.at[pl.ds(0, 3 * X * Y - 1)])
 
     @pl.when(zz > 1)
     def _():
         await_bytes(red_send.at[0], red_b)
 
-    @pl.when(zz < 2)
-    def _():
-        await_bytes(red_send.at[1], red_a.at[pl.ds(0, 7)])
+    @pl.when(zz == 0)
+    def _():
+        await_bytes(red_send.at[1], red_a.at[pl.ds(0, 8)])
+
+    @pl.when(zz == 1)
+    def _():
+        await_bytes(red_send.at[1], red_a.at[pl.ds(0, 6)])
 
     for copy in pair:
         copy.wait_send()
-    for copy in ends:
-        copy.wait()
+    keep.wait()
 
 
 def local(right_side, diag_blocks, block_values, block_cols, block_count, cell_diagonal):
@@ -465,6 +517,9 @@
         out_specs=hbm,
         scratch_shapes=[
             pltpu.VMEM((4, HALF, BS), F32),
+            pltpu.VMEM((2, 2 * HALF, BS), F32),
+            pltpu.VMEM((ITERS, 4, HALF, BS), F32),
+            pltpu.VMEM((ITERS, 2, HALF, BS), F32),
             pltpu.VMEM((4, HALF, BS), F32),
             pltpu.VMEM((2, BS, BS), F32),
             pltpu.VMEM((2, BS), F32),
@@ -482,17 +537,18 @@
             pltpu.VMEM((4 * (K + 1), HALF, BS), F32),
             pltpu.VMEM((ITERS, 2 * GROUP, HALF, BS), F32),
             pltpu.VMEM((ITERS, 2 * Y, 4, HALF, BS), F32),
-            pltpu.VMEM((2, 1, BS), F32),
-            pltpu.VMEM((X * Y * Z, 1, BS), F32),
+            pltpu.VMEM((3, 1, BS), F32),
+            pltpu.VMEM((2 * X * Y * Z, 1, BS), F32),
             pltpu.VMEM((1, 1, BS), F32),
-            pltpu.VMEM((2, 4, HALF, BS), F32),
+            pltpu.VMEM((1, 1, BS), F32),
+            pltpu.VMEM((2, 2, 2 * HALF, BS), F32),
             pltpu.SemaphoreType.DMA((7,)),
-            pltpu.SemaphoreType.DMA((7,)),
-            pltpu.SemaphoreType.DMA((7,)),
+            pltpu.SemaphoreType.DMA((8,)),
+            pltpu.SemaphoreType.DMA((8,)),
             pltpu.SemaphoreType.DMA((ITERS, 4)),
             pltpu.SemaphoreType.DMA((ITERS, 4)),
-            pltpu.SemaphoreType.DMA((2,)),
-            pltpu.SemaphoreType.DMA((2,)),
+            pltpu.SemaphoreType.DMA((3,)),
+            pltpu.SemaphoreType.DMA((4,)),
             pltpu.SemaphoreType.REGULAR((4,)),
         ],
         compiler_params=pltpu.CompilerParams(

time: 44.7 us -> 44 us (0.984)
  Pallas kernels: 42.5 us -> 41.5 us
    pallas_call x1, Pallas kernels: 42.5 us -> 41.5 us  [local(): pl.pallas_call(kernel, out_shape=jax.ShapeDtypeStruct((2, *right_side.sha...]
where the time goes in v5:
time: 44 us; the launch traced here: 43.5 us
  Pallas kernels  41.5 us (94%)
  local copies, waits for them, and re-layouts  1.35 us (3%)
  between operations  0.64 us (1%)
    pallas_call x1, Pallas kernels, local(): pl.pallas_call(kernel, out_shape=jax.ShapeDtypeStruct((2, *right_side.sha...  41.5 us
    squeeze x1, local copies, waits for them, and re-layouts, local(): return (both[0], both[1])  1.35 us

profile of v5, /device:TPU:1, one launch (start us, length us, event | category | flops | bytes accessed | tf_op | source)
XLA Modules:
  0.0 43.5 jit_solution(10804031800483087036)
XLA Ops:
  0.6 41.5 %cg.1 = f32[2,2,16,128]{3,2,1,0:T(8,128)} custom-call(f32[2,16,128]{2,1,0:T(8,128)} %right_ref.1, f32[2,128,128]{2,1,0:T(8,128)} %diag_ref.1, f32[2,4,128,128]{3,2,1,0:T(8,128)} %blocks_ref.1, s32[2,4]{1,0:T(2,128)} %cols_ref.1, f32[2,128]{1,0:T(2,128)} %celld_ref.1), custom_call_target="tpu_custom_call" | custom-call | tf_op jit(solution)/shard_map/cg/pallas_call | solution.py:513
  42.1 1.3 %slice_bitcast_fusion = (f32[2,16,128]{2,1,0:T(8,128)}, f32[2,16,128]{2,1,0:T(8,128)}) fusion(f32[2,2,16,128]{3,2,1,0:T(8,128)} %cg.1), kind=kLoop, calls=%fused_computation | loop fusion | bytes 65536 | tf_op jit(solution)/shard_map/squeeze | solution.py:559

commit v6 on v5

--- a/solution.py
+++ b/solution.py
@@ -60,8 +60,6 @@
         pltpu.make_async_copy(cols_ref, cols_v.at[core], local_sems.at[4]),
     ]
     loads.append(pltpu.make_async_copy(right_ref, rhs_all, local_sems.at[5]))
-    for load in loads:
-        load.start()
 
     win = (win_0, win_1, win_2)
     for window in win:
@@ -83,6 +81,9 @@
         pl.semaphore_signal(
             barrier, inc=1, device_id=(to_dom, to_sub - core), device_id_type=MESH
         )
+
+    for load in loads:
+        load.start()
 
     def to_partner(index, source, target):
         copy = pltpu.make_async_remote_copy(

time: 44 us -> 43.9 us (level)
  no operation moved by 1% of the time
where the time goes in v6:
time: 43.9 us; the launch traced here: 43.4 us
  Pallas kernels  41.4 us (94%)
  local copies, waits for them, and re-layouts  1.35 us (3%)
  between operations  0.64 us (1%)
    pallas_call x1, Pallas kernels, local(): pl.pallas_call(kernel, out_shape=jax.ShapeDtypeStruct((2, *right_side.sha...  41.4 us
    squeeze x1, local copies, waits for them, and re-layouts, local(): return (both[0], both[1])  1.35 us

profile of v6, /device:TPU:1, one launch (start us, length us, event | category | flops | bytes accessed | tf_op | source)
XLA Modules:
  0.0 43.4 jit_solution(8792366381999824613)
XLA Ops:
  0.6 41.4 %cg.1 = f32[2,2,16,128]{3,2,1,0:T(8,128)} custom-call(f32[2,16,128]{2,1,0:T(8,128)} %right_ref.1, f32[2,128,128]{2,1,0:T(8,128)} %diag_ref.1, f32[2,4,128,128]{3,2,1,0:T(8,128)} %blocks_ref.1, s32[2,4]{1,0:T(2,128)} %cols_ref.1, f32[2,128]{1,0:T(2,128)} %celld_ref.1), custom_call_target="tpu_custom_call" | custom-call | tf_op jit(solution)/shard_map/cg/pallas_call | solution.py:514
  42.1 1.3 %slice_bitcast_fusion = (f32[2,16,128]{2,1,0:T(8,128)}, f32[2,16,128]{2,1,0:T(8,128)}) fusion(f32[2,2,16,128]{3,2,1,0:T(8,128)} %cg.1), kind=kLoop, calls=%fused_computation | loop fusion | bytes 65536 | tf_op jit(solution)/shard_map/squeeze | solution.py:560
